TPU v7x, 256 devices: a whole 4x4x8 slice. The times are simulated.
256 devices in a mesh: blk: 16 (over x_hi, y, core), loop: 16 (over x_lo, z).
Axes of the slice: x: 4 (x_hi: 2, x_lo: 2; x = x_hi * 2 + x_lo), y: 4, z: 8, core: 2. Of those that a mesh axis runs over, the one named last changes fastest.
Arguments:
- points: bfloat16 [3072, 1024], P('blk'), may hold values from -6 to 6
- centroids: bfloat16 [262144, 1024], P(('blk', 'loop')), may hold values from -0.03125 to 0.03125
Outputs:
- new_centroids: bfloat16 [262144, 1024], P(('blk', 'loop'))
- normalizer: float32 [3072], P('blk')
All inputs are finite; a program needn't handle non-finite values.
Results may differ from a plain program's by a relative error of at most 0.0049.
Values may be sent and summed in bfloat16 or wider, within the bound.
A program may use at most 64 MiB of HBM per device.

v0:
```python
import jax
import jax.numpy as jnp
from jax import lax
from jax.sharding import PartitionSpec as P


def score_rows(rows, centroids):
    return (
        lax.dot_general(
            rows, centroids, (((1,), (1,)), ((), ())), preferred_element_type=jnp.float32
        )
        * 20.0
    )


def local_lse(scores):
    largest = jnp.max(scores, axis=1)
    return largest + jnp.log(jnp.sum(jnp.exp(scores - largest[:, None]), axis=1))


def statistics(scores, lse_rows, rows):
    weights = jnp.exp(scores - lse_rows[:, None])
    loads = jnp.sum(weights, axis=0)
    rounded = weights.astype(jnp.bfloat16)
    sums = lax.dot_general(
        rounded, rows, (((0,), (0,)), ((), ())), preferred_element_type=jnp.float32
    )
    return (loads, sums)


def per_device(points, centroids):
    count = points.shape[0]
    eta = float(centroids.shape[0] * lax.axis_size("loop")) / float(count)
    gathered = lax.all_gather(points, "blk", axis=0, tiled=True)
    scores = score_rows(gathered, centroids)
    partial_sums = local_lse(scores)
    peak = lax.pmax(partial_sums, ("blk", "loop"))
    total = lax.psum(jnp.exp(partial_sums - peak), ("blk", "loop"))
    normal_all = peak + jnp.log(total)
    loads, sums = statistics(scores, normal_all, gathered)
    fresh = (centroids.astype(jnp.float32) + eta * sums) / (1.0 + eta * loads)[:, None]
    own_rows = lax.dynamic_slice_in_dim(normal_all, lax.axis_index("blk") * count, count, 0)
    return (fresh.astype(jnp.bfloat16), own_rows)


def solution(mesh):
    placed = (P("blk", None), P(("blk", "loop"), None))
    return jax.shard_map(
        per_device,
        mesh=mesh,
        in_specs=placed,
        out_specs=(P(("blk", "loop"), None), P("blk")),
        check_vma=False,
    )
```

profile of v0, /device:TPU:1, one launch (start us, length us, event | category | flops | bytes accessed | tf_op | source)
XLA Modules:
  0.0 274.4 jit_solution(516589251914701975)
XLA Ops:
  7.2 0.0 all-gather.2.cloned.1.call-start
  7.2 0.7 all-gather.2.cloned.1.call-update
  7.9 76.3 %all-gather.2.cloned.1.call-done = bf16[3072,1024]{1,0:T(8,128)(2,1)} async-done(((bf16[192,1024]{1,0:T(8,128)(2,1)}), bf16[3072,1024]{1,0:T(8,128)(2,1)}) %all-gather.2.cloned.1.call-update) | async-done | bytes 6291472 | tf_op jit(solution)/shard_map/all_gather | solution.py:34
  84.2 9.5 %multiply_reduce_fusion = (f32[3072]{0:T(1024)S(1)}, f32[3072,1024]{0,1:T(8,128)S(1)}) fusion(bf16[3072,1024]{1,0:T(8,128)(2,1)} %all-gather.2.cloned.1.call-done, bf16[1024,1024]{1,0:T(8,128)(2,1)} %param.3), kind=kOutput, calls=%fused_computation.4 | convolution fusion | flops 6448739328 | bytes 20983808 | tf_op jit(solution)/shard_map/dot_general | solution.py:9
  93.7 0.0 copy-start
  93.7 4.6 %copy-done = f32[3072,1024]{0,1:T(8,128)} copy-done((f32[3072,1024]{0,1:T(8,128)}, f32[3072,1024]{0,1:T(8,128)S(1)}, u32[]{:S(2)}) %copy-start) | copy-done | bytes 12582936
  98.2 0.0 copy-start.2
  98.2 2.1 exponential_reduce_fusion
  100.3 74.9 %pmax.7 = f32[3072]{0:T(1024)S(1)} all-reduce(f32[3072]{0:T(1024)S(1)} %log_add_fusion.1), channel_id=1, replica_groups=mesh['blk'=16,'loop'=16] {'blk','loop'}, use_global_device_ids=true, to_apply=%region_2.0 | all-reduce | flops 3072 | bytes 24576 | tf_op jit(solution)/shard_map/pmax | solution.py:37
  175.3 74.1 %psum.7 = f32[3072]{0:T(1024)S(1)} all-reduce(f32[3072]{0:T(1024)S(1)} %subtract_exponential_fusion.1), channel_id=1, replica_groups=mesh['blk'=16,'loop'=16] {'blk','loop'}, use_global_device_ids=true, to_apply=%region_3.0 | all-reduce | flops 3072 | bytes 24576 | tf_op jit(solution)/shard_map/psum | solution.py:38
  249.4 0.0 copy-start.1
  249.4 6.9 %fusion = f32[1024]{0:T(1024)S(1)} fusion(f32[3072,1024]{0,1:T(8,128)} %copy-done, f32[3072]{0:T(1024)S(1)} %log_add_fusion), kind=kLoop, calls=%fused_computation.2 | loop fusion | flops 9436160 | bytes 12599296 | tf_op jit(solution)/shard_map/reduce_sum | solution.py:23
  256.3 0.6 dynamic_slice.3
  256.9 0.0 copy-done.2
  256.9 0.6 copy-done.1
  257.5 10.0 %divide_convert_fusion = bf16[1024,1024]{1,0:T(8,128)(2,1)} fusion(bf16[1024,1024]{1,0:T(8,128)(2,1)S(1)} %copy-done.2, bf16[3072,1024]{1,0:T(8,128)(2,1)} %all-gather.2.cloned.1.call-done, f32[3072,1024]{0,1:T(8,128)S(1)} %copy-done.1, f32[3072]{0:T(1024)S(1)} %log_add_fusion, f32[1024]{0:T(1024)S(1)} %multiply_add_fusion), kind=kOutput, calls=%fused_computation.8 | convolution fusion | flops 6457131008 | bytes 23085056 | tf_op jit(solution)/shard_map/dot_general | solution.py:25
  (4 shorter events, 0.0 us)
Async XLA Ops:
  7.2 77.0 %all-gather.2.cloned.1.call-start = ((), (), s32[]{:S(2)}) async-start(), calls=%async_computation | async-start | bytes 6684672 | tf_op jit(solution)/shard_map/all_gather | solution.py:34
  93.7 4.6 %copy-start = (f32[3072,1024]{0,1:T(8,128)}, f32[3072,1024]{0,1:T(8,128)S(1)}, u32[]{:S(2)}) copy-start(f32[3072,1024]{0,1:T(8,128)S(1)} %get-tuple-element.3) | copy-start | bytes 37748740
  98.2 158.7 %copy-start.2 = (bf16[1024,1024]{1,0:T(8,128)(2,1)S(1)}, bf16[1024,1024]{1,0:T(8,128)(2,1)}, u32[]{:S(2)}) copy-start(bf16[1024,1024]{1,0:T(8,128)(2,1)} %param.3) | copy-start | bytes 6291460
  249.4 8.2 %copy-start.1 = (f32[3072,1024]{0,1:T(8,128)S(1)}, f32[3072,1024]{0,1:T(8,128)}, u32[]{:S(2)}) copy-start(f32[3072,1024]{0,1:T(8,128)} %copy-done) | copy-start | bytes 37748740
Sparse Core Ops, SparseCore 0:
  10.8 73.3 all-gather.1
where the time goes:
time: 275 us; the launch traced here: 274 us
  blocking collectives  149 us (54%)
  waiting for transfers between devices  76.9 us (28%)
  matrix products  19.5 us (7%)
  between operations  14.1 us (5%)
  other arithmetic  9 us (3%)
  local copies, waits for them, and re-layouts  5.81 us (2%)
    all_gather x1, waiting for transfers between devices, per_device(): gathered = lax.all_gather(points, 'blk', axis=0, tiled=True)  76.3 us
    pmax x1, blocking collectives, per_device(): peak = lax.pmax(partial_sums, ('blk', 'loop'))  74.9 us
    psum x1, blocking collectives, per_device(): total = lax.psum(jnp.exp(partial_sums - peak), ('blk', 'loop'))  74.1 us
    dot_general x1, matrix products, statistics(): lax.dot_general(rounded, rows, (((0,), (0,)), ((), ())), preferred_elemen...  10 us
    dot_general x1, matrix products, score_rows(): lax.dot_general(rows, centroids, (((1,), (1,)), ((), ())), preferred_elem...  9.49 us
    reduce_sum x1, other arithmetic, statistics(): loads = jnp.sum(weights, axis=0)  6.89 us
  transfers between devices with their start and end apart: 1, of which 1 were waited for; matrix products, arithmetic and copies ran while one was open for 0% of the time, Pallas kernels for 0%

commit v1 on v0

v1 whole, which is shorter than its diff:
```python
import functools

import jax
import jax.numpy as jnp
from jax import lax
from jax.experimental import pallas as pl
from jax.experimental.pallas import tpu as pltpu
from jax.sharding import PartitionSpec as P

MESH = pl.DeviceIdType.MESH
NT = (((1,), (1,)), ((), ()))
LOG2E = 1.4426950408889634
LN2 = 0.6931471805599453
SCALE = 20.0 * LOG2E
NB = 16
CHUNKS = 6
AHEAD = 6


def merge(parts):
    top = jnp.max(parts, axis=0)
    return top + jnp.log2(jnp.sum(jnp.exp2(parts - top[None]), axis=0))


def kernel(
    eta, p_hbm, c_hbm, o_ref, n_ref,
    g, cent, s, acc, ld, ra, rb,
    load_sem, cent_sem, d1_send, d1_recv, sh_send, sh_recv, sib_send, sib_recv,
    a_send, a_recv, b_send, b_recv,
):
    count, width = p_hbm.shape
    rows = count // CHUNKS
    chunk = NB * rows
    lanes = 128
    groups = chunk // lanes
    half, quarter = width // 2, width // 4
    b = lax.axis_index("blk")
    l = lax.axis_index("loop")
    xh, y, c = b // 8, (b // 2) % 4, b % 2
    xl, z = l // 8, l % 8
    up, down, far = (y + 1) % 4, (y + 3) % 4, (y + 2) % 4
    ox, ol = 1 - xh, 1 - xl

    def blk_of(hi, yy):
        return (hi * 4 + yy) * 2 + c

    def shard_rows(hi, yy):
        return pl.ds(pl.multiple_of(c * (8 * rows) + (hi * 4 + yy) * rows, rows), rows)

    def cols_half(kind):
        return pl.ds(pl.multiple_of(kind * half, half), half)

    def cols_quarter(kind):
        return pl.ds(pl.multiple_of(kind * quarter, quarter), quarter)

    own = shard_rows(xh, y)
    for k in range(CHUNKS):
        pltpu.make_async_copy(p_hbm.at[pl.ds(k * rows, rows)], g.at[k, own], load_sem).start()
    cent_copy = pltpu.make_async_copy(c_hbm, cent, cent_sem)
    cent_copy.start()

    barrier = pltpu.get_barrier_semaphore()
    peers = [((b + j) % NB, l) for j in range(1, NB)]
    peers += [(b, (l + j) % NB) for j in range(1, NB)]
    peers += [(blk_of(ox, (y + j) % 4), ol * 8 + z) for j in range(4)]
    for peer in peers:
        pl.semaphore_signal(barrier, inc=1, device_id=peer, device_id_type=MESH)
    pl.semaphore_wait(barrier, len(peers))

    def wait_bytes(like, sem):
        pltpu.make_async_copy(like, like, sem).wait()

    my_half, my_quarter = (z + xl) % 2, (z + 2 * xl) % 4
    x_half, x_quarter = (z + ol) % 2, (z + 2 * ol) % 4
    x_loop = ol * 8 + z
    direct = [
        (blk_of(ox, down), x_loop, cols_quarter(x_quarter)),
        (blk_of(ox, up), x_loop, cols_quarter(x_quarter)),
        (blk_of(ox, far), x_loop, cols_quarter(x_quarter)),
        (blk_of(xh, far), l, cols_quarter(my_quarter)),
        (blk_of(xh, down), l, cols_half(my_half)),
        (blk_of(xh, up), l, cols_half(my_half)),
        (blk_of(ox, y), x_loop, cols_half(x_half)),
    ]
    z_up, z_down, x_same = xl * 8 + (z + 1) % 8, xl * 8 + (z + 7) % 8, ol * 8 + z
    arriving = [
        (shard_rows(ox, up), cols_quarter(my_quarter), (z_up, z_down, x_same)),
        (shard_rows(ox, down), cols_quarter(my_quarter), (z_up, z_down, x_same)),
        (shard_rows(ox, far), cols_quarter(my_quarter), (z_up, z_down, x_same)),
        (shard_rows(xh, far), cols_quarter(my_quarter), (z_up, z_down, x_same)),
        (shard_rows(xh, up), cols_half(my_half), (z_up,)),
        (shard_rows(xh, down), cols_half(my_half), (z_down,)),
        (shard_rows(ox, y), cols_half(my_half), (x_same,)),
    ]
    direct_bytes_rows = rows * 5 // 2
    share_bytes_rows = rows * 9 // 2

    def start_direct(k):
        for i, (tb, tl, cols) in enumerate(direct):
            pltpu.make_async_remote_copy(
                src_ref=g.at[k, own, cols], dst_ref=g.at[k, own, cols],
                send_sem=d1_send.at[k], recv_sem=d1_recv.at[k, i],
                device_id=(tb, tl), device_id_type=MESH,
            ).start()

    def share(k):
        for i, (rws, cols, targets) in enumerate(arriving):
            piece = g.at[k, rws, cols]
            wait_bytes(piece, d1_recv.at[k, i])
            for target in targets:
                pltpu.make_async_remote_copy(
                    src_ref=piece, dst_ref=piece,
                    send_sem=sh_send.at[k], recv_sem=sh_recv.at[k],
                    device_id=(b, target), device_id_type=MESH,
                ).start()

    mine = pl.ds(pl.multiple_of(c * (8 * rows), 8 * rows), 8 * rows)
    theirs = pl.ds(pl.multiple_of((1 - c) * (8 * rows), 8 * rows), 8 * rows)
    sibling = (b + 1 - 2 * c, l)

    def to_sibling(k):
        wait_bytes(p_hbm.at[pl.ds(0, share_bytes_rows)], sh_recv.at[k])
        pltpu.make_async_remote_copy(
            src_ref=g.at[k, mine], dst_ref=g.at[k, mine],
            send_sem=sib_send.at[k], recv_sem=sib_recv.at[k],
            device_id=sibling, device_id_type=MESH,
        ).start()

    tile = 256

    def scores(k):
        wait_bytes(g.at[k, theirs], sib_recv.at[k])
        top, total = None, None
        for m0 in range(0, width, tile):
            t = lax.dot_general(cent[m0:m0 + tile, :], g[k], NT, preferred_element_type=jnp.float32)
            s[k, m0:m0 + tile, :] = t
            t = t * SCALE
            high = jnp.max(jnp.max(t.reshape(tile // 8, 8, chunk), axis=0), axis=0, keepdims=True)
            new = high if top is None else jnp.maximum(top, high)
            part = jnp.sum(jnp.exp2(t - new).reshape(tile // 8, 8, chunk), axis=0)
            total = part if total is None else total * jnp.exp2(top - new) + part
            top = new
        lse = top + jnp.log2(jnp.sum(total, axis=0, keepdims=True))
        for q in range(groups):
            ra[k, l, q:q + 1, :] = lse[:, q * lanes:(q + 1) * lanes]
        for j in range(1, NB):
            pltpu.make_async_remote_copy(
                src_ref=ra.at[k, l], dst_ref=ra.at[k, l],
                send_sem=a_send.at[k], recv_sem=a_recv.at[k],
                device_id=(b, (l + j) % NB), device_id_type=MESH,
            ).start()

    def first_merge(k):
        wait_bytes(ra.at[k, pl.ds(0, NB - 1)], a_recv.at[k])
        rb[k, b] = merge(ra[k])
        for j in range(1, NB):
            pltpu.make_async_remote_copy(
                src_ref=rb.at[k, b], dst_ref=rb.at[k, b],
                send_sem=b_send.at[k], recv_sem=b_recv.at[k],
                device_id=((b + j) % NB, l), device_id_type=MESH,
            ).start()

    def sums(k):
        wait_bytes(rb.at[k, pl.ds(0, NB - 1)], b_recv.at[k])
        norm = merge(rb[k])
        n_ref[k] = norm * LN2
        line = jnp.concatenate([norm[q:q + 1, :] for q in range(groups)], axis=1)
        for m0 in range(0, width, tile):
            at = pl.ds(m0, tile)
            w = jnp.exp2(s[k, at, :] * SCALE - line)
            load = w[:, 0:lanes]
            for q in range(1, groups):
                load = load + w[:, q * lanes:(q + 1) * lanes]
            part = jnp.dot(w.astype(jnp.bfloat16), g[k], preferred_element_type=jnp.float32)
            if k > 0:
                load = load + ld[at, :]
                part = part + acc[at, :]
            if k < CHUNKS - 1:
                ld[at, :] = load
                acc[at, :] = part
            else:
                scale = 1.0 / (1.0 + eta * jnp.sum(load, axis=1, keepdims=True))
                fresh = (cent[at, :].astype(jnp.float32) + eta * part) * scale
                o_ref[at, :] = fresh.astype(jnp.bfloat16)

    wait_bytes(p_hbm, load_sem)
    for k in range(min(AHEAD, CHUNKS)):
        start_direct(k)
    for t in range(CHUNKS + 2):
        if t < CHUNKS:
            if t + AHEAD < CHUNKS:
                start_direct(t + AHEAD)
            share(t)
        if 0 <= t - 1 < CHUNKS:
            to_sibling(t - 1)
        if t == 2:
            cent_copy.wait()
        if 0 <= t - 2 < CHUNKS:
            scores(t - 2)
        if 0 <= t - 4 < CHUNKS:
            first_merge(t - 4)
    sums(0)
    first_merge(CHUNKS - 2)
    sums(1)
    first_merge(CHUNKS - 1)
    for k in range(2, CHUNKS):
        sums(k)

    for k in range(CHUNKS):
        wait_bytes(p_hbm.at[pl.ds(0, direct_bytes_rows)], d1_send.at[k])
        wait_bytes(p_hbm.at[pl.ds(0, share_bytes_rows)], sh_send.at[k])
        wait_bytes(g.at[k, mine], sib_send.at[k])
        wait_bytes(ra.at[k, pl.ds(0, NB - 1)], a_send.at[k])
        wait_bytes(rb.at[k, pl.ds(0, NB - 1)], b_send.at[k])


def per_device(points, centroids):
    count, width = points.shape
    held = centroids.shape[0]
    total = count * NB
    eta = float(held * NB * NB) / float(total)
    rows = count // CHUNKS
    chunk = NB * rows
    groups = chunk // 128
    dma = pltpu.SemaphoreType.DMA
    fresh, norm = pl.pallas_call(
        functools.partial(kernel, eta),
        out_shape=(
            jax.ShapeDtypeStruct((held, width), jnp.bfloat16),
            jax.ShapeDtypeStruct((CHUNKS, groups, 128), jnp.float32),
        ),
        in_specs=[pl.BlockSpec(memory_space=pl.ANY)] * 2,
        out_specs=(pl.BlockSpec(memory_space=pltpu.VMEM), pl.BlockSpec(memory_space=pltpu.VMEM)),
        scratch_shapes=[
            pltpu.VMEM((CHUNKS, chunk, width), jnp.bfloat16),
            pltpu.VMEM((held, width), jnp.bfloat16),
            pltpu.VMEM((CHUNKS, held, chunk), jnp.float32),
            pltpu.VMEM((held, width), jnp.float32),
            pltpu.VMEM((held, 128), jnp.float32),
            pltpu.VMEM((CHUNKS, NB, groups, 128), jnp.float32),
            pltpu.VMEM((CHUNKS, NB, groups, 128), jnp.float32),
            dma, dma,
            dma((CHUNKS,)), dma((CHUNKS, 7)),
            dma((CHUNKS,)), dma((CHUNKS,)),
            dma((CHUNKS,)), dma((CHUNKS,)),
            dma((CHUNKS,)), dma((CHUNKS,)),
            dma((CHUNKS,)), dma((CHUNKS,)),
        ],
        compiler_params=pltpu.CompilerParams(
            collective_id=0, has_side_effects=True, vmem_limit_bytes=48 * 1024 * 1024
        ),
        cost_estimate=pl.CostEstimate(
            flops=4 * total * held * width, bytes_accessed=6 * held * width, transcendentals=2 * total * held
        ),
    )(points, centroids)
    b = lax.axis_index("blk")
    start = (b % 2) * (8 * rows) + (b // 2) * rows
    own = lax.dynamic_slice_in_dim(norm.reshape(CHUNKS, chunk), start, rows, 1)
    return fresh, own.reshape(count)


def solution(mesh):
    placed = (P("blk", None), P(("blk", "loop"), None))
    return jax.shard_map(
        per_device,
        mesh=mesh,
        in_specs=placed,
        out_specs=(P(("blk", "loop"), None), P("blk")),
        check_vma=False,
    )
```

time: 275 us -> 58.7 us (0.21)
  blocking collectives: 149 us -> 0 us
  waiting for transfers between devices: 76.9 us -> 0 us
  Pallas kernels: 0 us -> 53.2 us
  matrix products: 19.5 us -> 0 us
  between operations: 14.1 us -> 0.68 us
  other arithmetic: 9 us -> 0 us
    all_gather x1 -> x0, waiting for transfers between devices: 76.3 us -> none  [per_device(): gathered = lax.all_gather(points, 'blk', axis=0, tiled=True)]
    pmax x1 -> x0, blocking collectives: 74.9 us -> none  [per_device(): peak = lax.pmax(partial_sums, ('blk', 'loop'))]
    psum x1 -> x0, blocking collectives: 74.1 us -> none  [per_device(): total = lax.psum(jnp.exp(partial_sums - peak), ('blk', 'loop'))]
    pallas_call x0 -> x1, Pallas kernels: none -> 53.2 us  [per_device(): pl.pallas_call(functools.partial(kernel, eta), out_shape=(jax.ShapeDtypeS...]
    dot_general x2 -> x0, matrix products: 19.5 us -> none  [the longest x1 10 us: statistics(): lax.dot_general(rounded, rows, (((0,), (0,)), ((), ())), preferred_elemen...]
    reduce_sum x2 -> x0, other arithmetic: 8.97 us -> none  [the longest x1 6.89 us: statistics(): loads = jnp.sum(weights, axis=0)]
  transfers between devices with their start and end apart: 1 -> 0, of which waited for: 1 -> 0; matrix products, arithmetic and copies ran while one was open for 0% -> 0% of each run, Pallas kernels for 0% -> 0%
where the time goes in v1:
time: 58.7 us; the launch traced here: 58.5 us
  Pallas kernels  53.2 us (91%)
  local copies, waits for them, and re-layouts  4.62 us (8%)
  between operations  0.68 us (1%)
    pallas_call x1, Pallas kernels, per_device(): pl.pallas_call(functools.partial(kernel, eta), out_shape=(jax.ShapeDtypeS...  53.2 us
    unnamed x6, local copies, waits for them, and re-layouts  3.9 us

profile of v1, /device:TPU:1, one launch (start us, length us, event | category | flops | bytes accessed | tf_op | source)
XLA Modules:
  0.0 58.5 jit_solution(10297228064033386707)
XLA Ops:
  0.7 0.0 copy-start
  0.7 1.6 %copy-done = bf16[1024,1024]{1,0:T(8,128)(2,1)S(1)} copy-done((bf16[1024,1024]{1,0:T(8,128)(2,1)S(1)}, bf16[1024,1024]{1,0:T(8,128)(2,1)}, u32[]{:S(2)}) %copy-start) | copy-done | bytes 2097176
  2.2 0.0 copy-start.1
  2.2 1.0 %copy-done.1 = bf16[192,1024]{1,0:T(8,128)(2,1)S(1)} copy-done((bf16[192,1024]{1,0:T(8,128)(2,1)S(1)}, bf16[192,1024]{1,0:T(8,128)(2,1)}, u32[]{:S(2)}) %copy-start.1) | copy-done | bytes 393240
  3.2 53.2 %shard_map.41 = (bf16[1024,1024]{1,0:T(8,128)(2,1)S(1)}, f32[6,4,128]{2,1,0:T(4,128)S(1)}) custom-call(bf16[192,1024]{1,0:T(8,128)(2,1)S(1)} %copy-done.1, bf16[1024,1024]{1,0:T(8,128)(2,1)S(1)} %copy-done), custom_call_target="tpu_custom_call" | custom-call | flops 12884901888 | bytes 6291456 | tf_op jit(solution)/shard_map/pallas_call | solution.py:226
  56.5 0.1 constant_dynamic-slice_fusion
  56.6 0.6 %reshape.11 = f32[192]{0:T(256)} reshape(f32[6,32]{1,0:T(8,128)S(1)} %constant_dynamic-slice_fusion) | data formatting | bytes 1536 | tf_op jit(solution)/shard_map/reshape | solution.py:259
  57.2 1.3 %copy.8 = bf16[1024,1024]{1,0:T(8,128)(2,1)} copy(bf16[1024,1024]{1,0:T(8,128)(2,1)S(1)} %get-tuple-element.8) | data formatting | bytes 4194304
  (1 shorter events, 0.0 us)
Async XLA Ops:
  0.7 1.6 %copy-start = (bf16[1024,1024]{1,0:T(8,128)(2,1)S(1)}, bf16[1024,1024]{1,0:T(8,128)(2,1)}, u32[]{:S(2)}) copy-start(bf16[1024,1024]{1,0:T(8,128)(2,1)} %c_hbm.1) | copy-start | bytes 6291460
  2.2 1.0 %copy-start.1 = (bf16[192,1024]{1,0:T(8,128)(2,1)S(1)}, bf16[192,1024]{1,0:T(8,128)(2,1)}, u32[]{:S(2)}) copy-start(bf16[192,1024]{1,0:T(8,128)(2,1)} %p_hbm.1) | copy-start | bytes 1179652

commit v2 on v0

v2 whole, which is shorter than its diff:
```python
import functools

import jax
import jax.numpy as jnp
from jax import lax
from jax.experimental import pallas as pl
from jax.experimental.pallas import tpu as pltpu
from jax.sharding import PartitionSpec as P

MESH = pl.DeviceIdType.MESH
NT = (((1,), (1,)), ((), ()))
LOG2E = 1.4426950408889634
LN2 = 0.6931471805599453
SCALE = 20.0 * LOG2E
NB = 16
SIZES = (64, 64, 64)
STARTS = (("Q", 0), ("Q", 1), ("Q", 2), ("F", 0), ("F", 1), ("F", 2))
STEPS = (
    ("share", 0), ("share", 1), ("share", 2),
    ("pass", 0), ("own", 0), ("sib", 0), ("tell", 0),
    ("pass", 1), ("own", 1), ("merge", 0), ("sib", 1), ("tell", 1),
    ("pass", 2), ("own", 2), ("sib", 2), ("tell", 2),
    ("merge", 1), ("sums", 0), ("merge", 2), ("sums", 1), ("sums", 2),
)

def merge(parts):
    top = jnp.max(parts, axis=0)
    return top + jnp.log2(jnp.sum(jnp.exp2(parts - top[None]), axis=0))


def kernel(eta, p_hbm, c_hbm, o_ref, n_ref, g, cent, acc, ld, *rest):
    chunks = len(SIZES)
    s, ra, rb = rest[:chunks], rest[chunks:2 * chunks], rest[2 * chunks:3 * chunks]
    (
        load_sem, cent_sem, q_recv, f_recv, d_send, sh_send, sh_recv, sib_send, sib_recv,
        a_send, a_recv, b_send, b_recv,
    ) = rest[3 * chunks:]
    count, width = p_hbm.shape
    held = cent.shape[0]
    lanes = 128
    quarter = width // 4
    b = lax.axis_index("blk")
    l = lax.axis_index("loop")
    xh, y, c = b // 8, (b // 2) % 4, b % 2
    xl, z = l // 8, l % 8
    up, down, far = (y + 1) % 4, (y + 3) % 4, (y + 2) % 4
    ox, ol = 1 - xh, 1 - xl
    sc = 1 - c
    shard = xh * 4 + y

    def blk_of(hi, yy):
        return (hi * 4 + yy) * 2 + c

    def first_row(k):
        return NB * sum(SIZES[:k])

    def shard_rows(k, hi, yy):
        rows = SIZES[k]
        return pl.ds(pl.multiple_of(first_row(k) + c * (8 * rows) + (hi * 4 + yy) * rows, 16), rows)

    def core_rows(k, core):
        rows = SIZES[k]
        return pl.ds(pl.multiple_of(first_row(k) + core * (8 * rows), 16), 8 * rows)

    def cols_quarter(kind):
        return pl.ds(pl.multiple_of(kind * quarter, quarter), quarter)

    for k, rows in enumerate(SIZES):
        pltpu.make_async_copy(
            p_hbm.at[pl.ds(sum(SIZES[:k]), rows)], g.at[shard_rows(k, xh, y)], load_sem
        ).start()
    cent_copy = pltpu.make_async_copy(c_hbm, cent, cent_sem)
    cent_copy.start()

    loop_order = [4, 12, 3, 5, 11, 13, 2, 6, 10, 14, 1, 7, 9, 15, 8]
    blk_order = [12, 4, 11, 13, 3, 5, 8, 9, 10, 14, 2, 6, 7, 15, 1]
    loop_peers = [(b, (l + j) % NB) for j in loop_order]
    blk_peers = [((b + j) % NB, l) for j in blk_order]
    x_loop = ol * 8 + z
    x_peers = [(blk_of(ox, (y + j) % 4), x_loop) for j in (2, 1, 3, 0)]
    barrier = pltpu.get_barrier_semaphore()
    for peer in loop_peers + blk_peers + x_peers:
        pl.semaphore_signal(barrier, inc=1, device_id=peer, device_id_type=MESH)
    pl.semaphore_wait(barrier, 2 * (NB - 1) + 4)

    def wait_bytes(like, sem):
        pltpu.make_async_copy(like, like, sem).wait()

    def send(piece, send_sem, recv_sem, peer):
        pltpu.make_async_remote_copy(
            src_ref=piece, dst_ref=piece, send_sem=send_sem, recv_sem=recv_sem,
            device_id=peer, device_id_type=MESH,
        ).start()

    my_quarter = cols_quarter((z + 2 * xl) % 4)
    x_quarter = cols_quarter((z + 2 * ol) % 4)
    parted = [
        ((blk_of(ox, down), x_loop), x_quarter, (ox, up)),
        ((blk_of(ox, up), x_loop), x_quarter, (ox, down)),
        ((blk_of(ox, far), x_loop), x_quarter, (ox, far)),
        ((blk_of(xh, far), l), my_quarter, (xh, far)),
    ]
    near = [(blk_of(xh, down), l), (blk_of(xh, up), l), (blk_of(ox, y), x_loop)]
    sharers = [(b, xl * 8 + (z + 1) % 8), (b, xl * 8 + (z + 7) % 8), (b, x_loop)]
    sibling = (b + 1 - 2 * c, l)

    def start_parted(k):
        for i, (peer, cols, _) in enumerate(parted):
            send(g.at[shard_rows(k, xh, y), cols], d_send.at[k], q_recv.at[k, i], peer)

    def start_near(k):
        for peer in near:
            send(g.at[shard_rows(k, xh, y)], d_send.at[k], f_recv.at[k], peer)

    def share(k):
        for i, (_, _, source) in enumerate(parted):
            piece = g.at[shard_rows(k, *source), my_quarter]
            wait_bytes(piece, q_recv.at[k, i])
            for peer in sharers:
                send(piece, sh_send.at[k], sh_recv.at[k], peer)

    def to_sibling(k):
        wait_bytes(g.at[pl.ds(0, 3 * SIZES[k])], f_recv.at[k])
        wait_bytes(g.at[pl.ds(0, 3 * SIZES[k])], sh_recv.at[k])
        send(g.at[core_rows(k, c)], sib_send.at[k], sib_recv.at[k], sibling)

    tile = 256

    def scores(k, core):
        part = 8 * SIZES[k]
        top, total = None, None
        for m0 in range(0, held, tile):
            t = lax.dot_general(
                cent[m0:m0 + tile, :], g[core_rows(k, core), :], NT, preferred_element_type=jnp.float32
            )
            s[k][core, m0:m0 + tile, :] = t
            t = t * SCALE
            high = jnp.max(jnp.max(t.reshape(tile // 8, 8, part), axis=0), axis=0, keepdims=True)
            new = high if top is None else jnp.maximum(top, high)
            add = jnp.sum(jnp.exp2(t - new).reshape(tile // 8, 8, part), axis=0)
            total = add if total is None else total * jnp.exp2(top - new) + add
            top = new
        lse = top + jnp.log2(jnp.sum(total, axis=0, keepdims=True))
        for q in range(part // lanes):
            ra[k][l, core, q:q + 1, :] = lse[:, q * lanes:(q + 1) * lanes]

    def sibling_scores(k):
        wait_bytes(g.at[core_rows(k, sc)], sib_recv.at[k])
        scores(k, sc)

    def tell(k):
        for peer in loop_peers:
            send(ra[k].at[l], a_send.at[k], a_recv.at[k], peer)

    def first_merge(k):
        wait_bytes(ra[k].at[pl.ds(0, NB - 1)], a_recv.at[k])
        rb[k][b] = merge(ra[k][...])
        for peer in blk_peers:
            send(rb[k].at[b], b_send.at[k], b_recv.at[k], peer)

    def sums(k):
        rows = SIZES[k]
        part = 8 * rows
        groups = part // lanes
        wait_bytes(rb[k].at[pl.ds(0, NB - 1)], b_recv.at[k])
        norm = merge(rb[k][...])
        lines = [
            jnp.concatenate([norm[h, q:q + 1, :] for q in range(groups)], axis=1) for h in range(2)
        ]
        for m0 in range(0, held, tile):
            at = pl.ds(m0, tile)
            w = jnp.concatenate([jnp.exp2(s[k][h, at, :] * SCALE - lines[h]) for h in range(2)], axis=1)
            load = w[:, 0:lanes]
            for q in range(1, 2 * groups):
                load = load + w[:, q * lanes:(q + 1) * lanes]
            add = jnp.dot(
                w.astype(jnp.bfloat16), g[pl.ds(first_row(k), NB * rows), :],
                preferred_element_type=jnp.float32,
            )
            if k > 0:
                load = load + ld[at, :]
                add = add + acc[at, :]
            if k < chunks - 1:
                ld[at, :] = load
                acc[at, :] = add
            else:
                scale = 1.0 / (1.0 + eta * jnp.sum(load, axis=1, keepdims=True))
                fresh = (cent[at, :].astype(jnp.float32) + eta * add) * scale
                o_ref[at, :] = fresh.astype(jnp.bfloat16)
        line = jnp.where(c == 0, lines[0], lines[1])
        for bit in range(3):
            turned = pltpu.roll(line, part - (rows << bit), 1)
            line = jnp.where((shard // (1 << bit)) % 2 == 1, turned, line)
        start = sum(SIZES[:k])
        n_ref[:, start:start + rows] = line[:, 0:rows] * LN2

    wait_bytes(p_hbm, load_sem)
    for kind, k in STARTS:
        start_parted(k) if kind == "Q" else start_near(k)
    cent_copy.wait()
    actions = dict(
        share=share, own=lambda k: scores(k, c), sib=sibling_scores, tell=tell,
        merge=first_merge, sums=sums,
    )
    actions["pass"] = to_sibling
    for kind, k in STEPS:
        actions[kind](k)

    for k, rows in enumerate(SIZES):
        wait_bytes(g.at[pl.ds(0, 4 * rows)], d_send.at[k])
        wait_bytes(g.at[pl.ds(0, 3 * rows)], sh_send.at[k])
        wait_bytes(g.at[core_rows(k, c)], sib_send.at[k])
        wait_bytes(ra[k].at[pl.ds(0, NB - 1)], a_send.at[k])
        wait_bytes(rb[k].at[pl.ds(0, NB - 1)], b_send.at[k])


def per_device(points, centroids):
    count, width = points.shape
    held = centroids.shape[0]
    total = count * NB
    eta = float(held * NB * NB) / float(total)
    chunks = len(SIZES)
    dma = pltpu.SemaphoreType.DMA
    hbm = pl.BlockSpec(memory_space=pltpu.HBM)
    vmem = pl.BlockSpec(memory_space=pltpu.VMEM)
    stats = [pltpu.VMEM((NB, 2, 8 * rows // 128, 128), jnp.float32) for rows in SIZES]
    each = dma((chunks,))
    fresh, norm = pl.pallas_call(
        functools.partial(kernel, eta),
        out_shape=(
            jax.ShapeDtypeStruct((held, width), jnp.bfloat16),
            jax.ShapeDtypeStruct((1, count), jnp.float32),
        ),
        in_specs=[hbm, hbm],
        out_specs=(vmem, vmem),
        scratch_shapes=[
            pltpu.VMEM((total, width), jnp.bfloat16),
            pltpu.VMEM((held, width), jnp.bfloat16),
            pltpu.VMEM((held, width), jnp.float32),
            pltpu.VMEM((held, 128), jnp.float32),
            *[pltpu.VMEM((2, held, 8 * rows), jnp.float32) for rows in SIZES],
            *stats, *stats,
            dma, dma,
            dma((chunks, 4)), each, each,
            each, each, each, each,
            each, each, each, each,
        ],
        compiler_params=pltpu.CompilerParams(
            collective_id=0, has_side_effects=True, vmem_limit_bytes=51 * 1024 * 1024
        ),
        cost_estimate=pl.CostEstimate(
            flops=4 * total * held * width, bytes_accessed=6 * held * width, transcendentals=2 * total * held
        ),
    )(points, centroids)
    return fresh, norm.reshape(count)


def solution(mesh):
    placed = (P("blk", None), P(("blk", "loop"), None))
    return jax.shard_map(
        per_device,
        mesh=mesh,
        in_specs=placed,
        out_specs=(P(("blk", "loop"), None), P("blk")),
        check_vma=False,
    )
```

time: 275 us -> 54 us (0.20)
  blocking collectives: 149 us -> 0 us
  waiting for transfers between devices: 76.9 us -> 0 us
  Pallas kernels: 0 us -> 50.3 us
  matrix products: 19.5 us -> 0 us
  between operations: 14.1 us -> 0.65 us
  other arithmetic: 9 us -> 0 us
  local copies, waits for them, and re-layouts: 5.81 us -> 2.87 us
    all_gather x1 -> x0, waiting for transfers between devices: 76.3 us -> none  [per_device(): gathered = lax.all_gather(points, 'blk', axis=0, tiled=True)]
    pmax x1 -> x0, blocking collectives: 74.9 us -> none  [per_device(): peak = lax.pmax(partial_sums, ('blk', 'loop'))]
    psum x1 -> x0, blocking collectives: 74.1 us -> none  [per_device(): total = lax.psum(jnp.exp(partial_sums - peak), ('blk', 'loop'))]
    pallas_call x0 -> x1, Pallas kernels: none -> 50.3 us  [per_device(): pl.pallas_call(functools.partial(kernel, eta), out_shape=(jax.ShapeDtypeS...]
    dot_general x2 -> x0, matrix products: 19.5 us -> none  [the longest x1 10 us: statistics(): lax.dot_general(rounded, rows, (((0,), (0,)), ((), ())), preferred_elemen...]
    reduce_sum x2 -> x0, other arithmetic: 8.97 us -> none  [the longest x1 6.89 us: statistics(): loads = jnp.sum(weights, axis=0)]
  transfers between devices with their start and end apart: 1 -> 0, of which waited for: 1 -> 0; matrix products, arithmetic and copies ran while one was open for 0% -> 0% of each run, Pallas kernels for 0% -> 0%
where the time goes in v2:
time: 54 us; the launch traced here: 53.8 us
  Pallas kernels  50.3 us (93%)
  local copies, waits for them, and re-layouts  2.87 us (5%)
  between operations  0.65 us (1%)
    pallas_call x1, Pallas kernels, per_device(): pl.pallas_call(functools.partial(kernel, eta), out_shape=(jax.ShapeDtypeS...  50.3 us
    unnamed x4, local copies, waits for them, and re-layouts  2.87 us

profile of v2, /device:TPU:1, one launch (start us, length us, event | category | flops | bytes accessed | tf_op | source)
XLA Modules:
  0.0 53.8 jit_solution(13731094192512754938)
XLA Ops:
  0.6 0.0 copy-start
  0.6 1.0 %copy-done = bf16[192,1024]{1,0:T(8,128)(2,1)S(1)} copy-done((bf16[192,1024]{1,0:T(8,128)(2,1)S(1)}, bf16[192,1024]{1,0:T(8,128)(2,1)}, u32[]{:S(2)}) %copy-start) | copy-done | bytes 393240
  1.6 50.3 %shard_map.41 = (bf16[1024,1024]{1,0:T(8,128)(2,1)S(1)}, f32[1,192]{1,0:T(1,128)S(1)}) custom-call(bf16[192,1024]{1,0:T(8,128)(2,1)S(1)} %copy-done, bf16[1024,1024]{1,0:T(8,128)(2,1)} %c_hbm.1), custom_call_target="tpu_custom_call" | custom-call | flops 12884901888 | bytes 6291456 | tf_op jit(solution)/shard_map/pallas_call | solution.py:228
  52.0 1.3 %copy.6 = bf16[1024,1024]{1,0:T(8,128)(2,1)} copy(bf16[1024,1024]{1,0:T(8,128)(2,1)S(1)} %get-tuple-element.8) | data formatting | bytes 4194304
  53.3 0.6 %copy.7 = f32[192]{0:T(256)} copy(f32[192]{0:T(256)S(1)} %bitcast.1) | data formatting | bytes 1536
Async XLA Ops:
  0.6 1.0 %copy-start = (bf16[192,1024]{1,0:T(8,128)(2,1)S(1)}, bf16[192,1024]{1,0:T(8,128)(2,1)}, u32[]{:S(2)}) copy-start(bf16[192,1024]{1,0:T(8,128)(2,1)} %p_hbm.1) | copy-start | bytes 1179652

commit v3 on v2

--- a/solution.py
+++ b/solution.py
@@ -16,11 +16,27 @@
 SIZES = (64, 64, 64)
 STARTS = (("Q", 0), ("Q", 1), ("Q", 2), ("F", 0), ("F", 1), ("F", 2))
 STEPS = (
-    ("share", 0), ("share", 1), ("share", 2),
-    ("pass", 0), ("own", 0), ("sib", 0), ("tell", 0),
-    ("pass", 1), ("own", 1), ("merge", 0), ("sib", 1), ("tell", 1),
-    ("pass", 2), ("own", 2), ("sib", 2), ("tell", 2),
-    ("merge", 1), ("sums", 0), ("merge", 2), ("sums", 1), ("sums", 2),
+    ("share", 0),
+    ("share", 1),
+    ("share", 2),
+    ("pass", 0),
+    ("own", 0),
+    ("pass", 1),
+    ("sib", 0),
+    ("tell", 0),
+    ("own", 1),
+    ("pass", 2),
+    ("sib", 1),
+    ("tell", 1),
+    ("own", 2),
+    ("sib", 2),
+    ("tell", 2),
+    ("merge", 0),
+    ("merge", 1),
+    ("merge", 2),
+    ("sums", 0),
+    ("sums", 1),
+    ("sums", 2),
 )
 
 def merge(parts):
@@ -65,13 +81,6 @@
     def cols_quarter(kind):
         return pl.ds(pl.multiple_of(kind * quarter, quarter), quarter)
 
-    for k, rows in enumerate(SIZES):
-        pltpu.make_async_copy(
-            p_hbm.at[pl.ds(sum(SIZES[:k]), rows)], g.at[shard_rows(k, xh, y)], load_sem
-        ).start()
-    cent_copy = pltpu.make_async_copy(c_hbm, cent, cent_sem)
-    cent_copy.start()
-
     loop_order = [4, 12, 3, 5, 11, 13, 2, 6, 10, 14, 1, 7, 9, 15, 8]
     blk_order = [12, 4, 11, 13, 3, 5, 8, 9, 10, 14, 2, 6, 7, 15, 1]
     loop_peers = [(b, (l + j) % NB) for j in loop_order]
@@ -79,16 +88,23 @@
     x_loop = ol * 8 + z
     x_peers = [(blk_of(ox, (y + j) % 4), x_loop) for j in (2, 1, 3, 0)]
     barrier = pltpu.get_barrier_semaphore()
-    for peer in loop_peers + blk_peers + x_peers:
+    for peer in x_peers + blk_peers[::-1] + loop_peers[::-1]:
         pl.semaphore_signal(barrier, inc=1, device_id=peer, device_id_type=MESH)
+    for k, rows in enumerate(SIZES):
+        pltpu.make_async_copy(
+            p_hbm.at[pl.ds(sum(SIZES[:k]), rows)], g.at[shard_rows(k, xh, y)], load_sem
+        ).start()
+    cent_copy = pltpu.make_async_copy(c_hbm, cent, cent_sem)
+    cent_copy.start()
+
     pl.semaphore_wait(barrier, 2 * (NB - 1) + 4)
 
     def wait_bytes(like, sem):
         pltpu.make_async_copy(like, like, sem).wait()
 
-    def send(piece, send_sem, recv_sem, peer):
+    def send(piece, send_sem, recv_sem, peer, source=None):
         pltpu.make_async_remote_copy(
-            src_ref=piece, dst_ref=piece, send_sem=send_sem, recv_sem=recv_sem,
+            src_ref=piece if source is None else source, dst_ref=piece, send_sem=send_sem, recv_sem=recv_sem,
             device_id=peer, device_id_type=MESH,
         ).start()
 
@@ -104,13 +120,16 @@
     sharers = [(b, xl * 8 + (z + 1) % 8), (b, xl * 8 + (z + 7) % 8), (b, x_loop)]
     sibling = (b + 1 - 2 * c, l)
 
+    def own_rows(k):
+        return p_hbm.at[pl.ds(sum(SIZES[:k]), SIZES[k])]
+
     def start_parted(k):
         for i, (peer, cols, _) in enumerate(parted):
-            send(g.at[shard_rows(k, xh, y), cols], d_send.at[k], q_recv.at[k, i], peer)
+            send(g.at[shard_rows(k, xh, y), cols], d_send.at[k], q_recv.at[k, i], peer, own_rows(k).at[:, cols])
 
     def start_near(k):
         for peer in near:
-            send(g.at[shard_rows(k, xh, y)], d_send.at[k], f_recv.at[k], peer)
+            send(g.at[shard_rows(k, xh, y)], d_send.at[k], f_recv.at[k], peer, own_rows(k))
 
     def share(k):
         for i, (_, _, source) in enumerate(parted):
@@ -120,9 +139,12 @@
                 send(piece, sh_send.at[k], sh_recv.at[k], peer)
 
     def to_sibling(k):
+        wait_bytes(g.at[pl.ds(0, 3 * SIZES[k])], sh_recv.at[k])
+        for place in ((ox, up), (ox, down), (ox, far), (xh, far)):
+            send(g.at[shard_rows(k, *place)], sib_send.at[k], sib_recv.at[k], sibling)
         wait_bytes(g.at[pl.ds(0, 3 * SIZES[k])], f_recv.at[k])
-        wait_bytes(g.at[pl.ds(0, 3 * SIZES[k])], sh_recv.at[k])
-        send(g.at[core_rows(k, c)], sib_send.at[k], sib_recv.at[k], sibling)
+        for place in ((xh, y), (xh, up), (xh, down), (ox, y)):
+            send(g.at[shard_rows(k, *place)], sib_send.at[k], sib_recv.at[k], sibling)
 
     tile = 256
 
@@ -133,14 +155,16 @@
             t = lax.dot_general(
                 cent[m0:m0 + tile, :], g[core_rows(k, core), :], NT, preferred_element_type=jnp.float32
             )
+            t = t * SCALE
             s[k][core, m0:m0 + tile, :] = t
-            t = t * SCALE
-            high = jnp.max(jnp.max(t.reshape(tile // 8, 8, part), axis=0), axis=0, keepdims=True)
+            t = t.reshape(tile // 8, 8, part)
+            high = jnp.max(t, axis=0)
             new = high if top is None else jnp.maximum(top, high)
-            add = jnp.sum(jnp.exp2(t - new).reshape(tile // 8, 8, part), axis=0)
+            add = jnp.sum(jnp.exp2(t - new[None]), axis=0)
             total = add if total is None else total * jnp.exp2(top - new) + add
             top = new
-        lse = top + jnp.log2(jnp.sum(total, axis=0, keepdims=True))
+        peak = jnp.max(top, axis=0, keepdims=True)
+        lse = peak + jnp.log2(jnp.sum(total * jnp.exp2(top - peak), axis=0, keepdims=True))
         for q in range(part // lanes):
             ra[k][l, core, q:q + 1, :] = lse[:, q * lanes:(q + 1) * lanes]
 
@@ -169,7 +193,7 @@
         ]
         for m0 in range(0, held, tile):
             at = pl.ds(m0, tile)
-            w = jnp.concatenate([jnp.exp2(s[k][h, at, :] * SCALE - lines[h]) for h in range(2)], axis=1)
+            w = jnp.concatenate([jnp.exp2(s[k][h, at, :] - lines[h]) for h in range(2)], axis=1)
             load = w[:, 0:lanes]
             for q in range(1, 2 * groups):
                 load = load + w[:, q * lanes:(q + 1) * lanes]
@@ -194,9 +218,9 @@
         start = sum(SIZES[:k])
         n_ref[:, start:start + rows] = line[:, 0:rows] * LN2
 
-    wait_bytes(p_hbm, load_sem)
     for kind, k in STARTS:
         start_parted(k) if kind == "Q" else start_near(k)
+    wait_bytes(p_hbm, load_sem)
     cent_copy.wait()
     actions = dict(
         share=share, own=lambda k: scores(k, c), sib=sibling_scores, tell=tell,

time: 54 us -> 50.2 us (0.930)
  Pallas kernels: 50.3 us -> 46.5 us
    pallas_call x1, Pallas kernels: 50.3 us -> 46.5 us  [per_device(): pl.pallas_call(functools.partial(kernel, eta), out_shape=(jax.ShapeDtypeS...]
where the time goes in v3:
time: 50.2 us; the launch traced here: 50 us
  Pallas kernels  46.5 us (93%)
  local copies, waits for them, and re-layouts  2.87 us (6%)
  between operations  0.65 us (1%)
    pallas_call x1, Pallas kernels, per_device(): pl.pallas_call(functools.partial(kernel, eta), out_shape=(jax.ShapeDtypeS...  46.5 us
    unnamed x4, local copies, waits for them, and re-layouts  2.87 us

profile of v3, /device:TPU:1, one launch (start us, length us, event | category | flops | bytes accessed | tf_op | source)
XLA Modules:
  0.0 50.0 jit_solution(14744763730844445396)
XLA Ops:
  0.6 0.0 copy-start
  0.6 1.0 %copy-done = bf16[192,1024]{1,0:T(8,128)(2,1)S(1)} copy-done((bf16[192,1024]{1,0:T(8,128)(2,1)S(1)}, bf16[192,1024]{1,0:T(8,128)(2,1)}, u32[]{:S(2)}) %copy-start) | copy-done | bytes 393240
  1.6 46.5 %shard_map.41 = (bf16[1024,1024]{1,0:T(8,128)(2,1)S(1)}, f32[1,192]{1,0:T(1,128)S(1)}) custom-call(bf16[192,1024]{1,0:T(8,128)(2,1)S(1)} %copy-done, bf16[1024,1024]{1,0:T(8,128)(2,1)} %c_hbm.1), custom_call_target="tpu_custom_call" | custom-call | flops 12884901888 | bytes 6291456 | tf_op jit(solution)/shard_map/pallas_call | solution.py:252
  48.2 1.3 %copy.6 = bf16[1024,1024]{1,0:T(8,128)(2,1)} copy(bf16[1024,1024]{1,0:T(8,128)(2,1)S(1)} %get-tuple-element.8) | data formatting | bytes 4194304
  49.5 0.6 %copy.7 = f32[192]{0:T(256)} copy(f32[192]{0:T(256)S(1)} %bitcast.1) | data formatting | bytes 1536
Async XLA Ops:
  0.6 1.0 %copy-start = (bf16[192,1024]{1,0:T(8,128)(2,1)S(1)}, bf16[192,1024]{1,0:T(8,128)(2,1)}, u32[]{:S(2)}) copy-start(bf16[192,1024]{1,0:T(8,128)(2,1)} %p_hbm.1) | copy-start | bytes 1179652

commit v4 on v3

--- a/solution.py
+++ b/solution.py
@@ -12,6 +12,7 @@
 LOG2E = 1.4426950408889634
 LN2 = 0.6931471805599453
 SCALE = 20.0 * LOG2E
+WRITES = 4
 NB = 16
 SIZES = (64, 64, 64)
 STARTS = (("Q", 0), ("Q", 1), ("Q", 2), ("F", 0), ("F", 1), ("F", 2))
@@ -238,6 +239,18 @@
         wait_bytes(rb[k].at[pl.ds(0, NB - 1)], b_send.at[k])
 
 
+def write_out(fresh, norm, fresh_out, norm_out, sems):
+    rows = fresh.shape[0] // WRITES
+    copies = [pltpu.make_async_copy(norm, norm_out, sems.at[WRITES])]
+    for i in range(WRITES):
+        at = pl.ds(i * rows, rows)
+        copies.append(pltpu.make_async_copy(fresh.at[at], fresh_out.at[at], sems.at[i]))
+    for copy in copies:
+        copy.start()
+    for copy in copies:
+        copy.wait()
+
+
 def per_device(points, centroids):
     count, width = points.shape
     held = centroids.shape[0]
@@ -247,6 +260,7 @@
     dma = pltpu.SemaphoreType.DMA
     hbm = pl.BlockSpec(memory_space=pltpu.HBM)
     vmem = pl.BlockSpec(memory_space=pltpu.VMEM)
+    anywhere = pl.BlockSpec(memory_space=pl.ANY)
     stats = [pltpu.VMEM((NB, 2, 8 * rows // 128, 128), jnp.float32) for rows in SIZES]
     each = dma((chunks,))
     fresh, norm = pl.pallas_call(
@@ -276,6 +290,17 @@
             flops=4 * total * held * width, bytes_accessed=6 * held * width, transcendentals=2 * total * held
         ),
     )(points, centroids)
+    fresh, norm = pl.pallas_call(
+        write_out,
+        out_shape=(
+            jax.ShapeDtypeStruct((held, width), jnp.bfloat16),
+            jax.ShapeDtypeStruct((1, count), jnp.float32),
+        ),
+        in_specs=[vmem, vmem],
+        out_specs=(anywhere, anywhere),
+        scratch_shapes=[dma((WRITES + 1,))],
+        compiler_params=pltpu.CompilerParams(vmem_limit_bytes=8 * 1024 * 1024),
+    )(fresh, norm)
     return fresh, norm.reshape(count)
 
 

time: 50.2 us -> 49.8 us (level)
  local copies, waits for them, and re-layouts: 2.87 us -> 0.99 us
  Pallas kernels: 46.5 us -> 47.9 us
    unnamed x4 -> x2, local copies, waits for them, and re-layouts: 2.87 us -> 0.99 us
    pallas_call x0 -> x1, Pallas kernels: none -> 1.36 us  [per_device(): pl.pallas_call(write_out, out_shape=(jax.ShapeDtypeStruct((held, width),...]
where the time goes in v4:
time: 49.8 us; the launch traced here: 49.7 us
  Pallas kernels  47.9 us (96%)
  local copies, waits for them, and re-layouts  0.99 us (2%)
  between operations  0.81 us (2%)
    pallas_call x1, Pallas kernels, per_device(): pl.pallas_call(functools.partial(kernel, eta), out_shape=(jax.ShapeDtypeS...  46.5 us
    pallas_call x1, Pallas kernels, per_device(): pl.pallas_call(write_out, out_shape=(jax.ShapeDtypeStruct((held, width),...  1.36 us

profile of v4, /device:TPU:1, one launch (start us, length us, event | category | flops | bytes accessed | tf_op | source)
XLA Modules:
  0.0 49.7 jit_solution(14253194406751261490)
XLA Ops:
  0.6 0.0 copy-start
  0.6 1.0 %copy-done = bf16[192,1024]{1,0:T(8,128)(2,1)S(1)} copy-done((bf16[192,1024]{1,0:T(8,128)(2,1)S(1)}, bf16[192,1024]{1,0:T(8,128)(2,1)}, u32[]{:S(2)}) %copy-start) | copy-done | bytes 393240
  1.6 46.5 %shard_map.41 = (bf16[1024,1024]{1,0:T(8,128)(2,1)S(1)}, f32[1,192]{1,0:T(1,128)S(1)}) custom-call(bf16[192,1024]{1,0:T(8,128)(2,1)S(1)} %copy-done, bf16[1024,1024]{1,0:T(8,128)(2,1)} %c_hbm.1), custom_call_target="tpu_custom_call" | custom-call | flops 12884901888 | bytes 6291456 | tf_op jit(solution)/shard_map/pallas_call | solution.py:266
  48.2 1.4 %shard_map.42 = (bf16[1024,1024]{1,0:T(8,128)(2,1)}, f32[1,192]{1,0:T(1,128)}) custom-call(bf16[1024,1024]{1,0:T(8,128)(2,1)S(1)} %get-tuple-element.6.fresh, f32[1,192]{1,0:T(1,128)S(1)} %get-tuple-element.7.norm), custom_call_target="tpu_custom_call" | custom-call | tf_op jit(solution)/shard_map/pallas_call | solution.py:293
Async XLA Ops:
  0.6 1.0 %copy-start = (bf16[192,1024]{1,0:T(8,128)(2,1)S(1)}, bf16[192,1024]{1,0:T(8,128)(2,1)}, u32[]{:S(2)}) copy-start(bf16[192,1024]{1,0:T(8,128)(2,1)} %p_hbm.1) | copy-start | bytes 1179652

commit v5 on v4

--- a/solution.py
+++ b/solution.py
@@ -13,14 +13,20 @@
 LN2 = 0.6931471805599453
 SCALE = 20.0 * LOG2E
 WRITES = 4
+GREETINGS = 4
 NB = 16
 SIZES = (64, 64, 64)
 STARTS = (("Q", 0), ("Q", 1), ("Q", 2), ("F", 0), ("F", 1), ("F", 2))
 STEPS = (
+    ("greet", 0),
     ("share", 0),
+    ("greet", 1),
     ("share", 1),
+    ("greet", 2),
     ("share", 2),
+    ("greet", 3),
     ("pass", 0),
+    ("greet", 4),
     ("own", 0),
     ("pass", 1),
     ("sib", 0),
@@ -49,7 +55,7 @@
     chunks = len(SIZES)
     s, ra, rb = rest[:chunks], rest[chunks:2 * chunks], rest[2 * chunks:3 * chunks]
     (
-        load_sem, cent_sem, q_recv, f_recv, d_send, sh_send, sh_recv, sib_send, sib_recv,
+        met, load_sem, cent_sem, q_recv, f_recv, d_send, sh_send, sh_recv, sib_send, sib_recv,
         a_send, a_recv, b_send, b_recv,
     ) = rest[3 * chunks:]
     count, width = p_hbm.shape
@@ -89,8 +95,13 @@
     x_loop = ol * 8 + z
     x_peers = [(blk_of(ox, (y + j) % 4), x_loop) for j in (2, 1, 3, 0)]
     barrier = pltpu.get_barrier_semaphore()
-    for peer in x_peers + blk_peers[::-1] + loop_peers[::-1]:
+    z_up, z_down = (b, xl * 8 + (z + 1) % 8), (b, xl * 8 + (z + 7) % 8)
+    sibling = (b + 1 - 2 * c, l)
+    close = [z_up, z_down, (b, x_loop), sibling]
+    first = close + x_peers + [(blk_of(xh, far), l), (blk_of(xh, up), l), (blk_of(xh, down), l)]
+    for peer in first:
         pl.semaphore_signal(barrier, inc=1, device_id=peer, device_id_type=MESH)
+
     for k, rows in enumerate(SIZES):
         pltpu.make_async_copy(
             p_hbm.at[pl.ds(sum(SIZES[:k]), rows)], g.at[shard_rows(k, xh, y)], load_sem
@@ -98,7 +109,14 @@
     cent_copy = pltpu.make_async_copy(c_hbm, cent, cent_sem)
     cent_copy.start()
 
-    pl.semaphore_wait(barrier, 2 * (NB - 1) + 4)
+    pl.semaphore_wait(barrier, len(first))
+
+    def greet(turn):
+        if turn > 0:
+            pl.semaphore_wait(met.at[turn - 1], len(close))
+        if turn < GREETINGS:
+            for peer in close:
+                pl.semaphore_signal(met.at[turn], inc=1, device_id=peer, device_id_type=MESH)
 
     def wait_bytes(like, sem):
         pltpu.make_async_copy(like, like, sem).wait()
@@ -118,8 +136,7 @@
         ((blk_of(xh, far), l), my_quarter, (xh, far)),
     ]
     near = [(blk_of(xh, down), l), (blk_of(xh, up), l), (blk_of(ox, y), x_loop)]
-    sharers = [(b, xl * 8 + (z + 1) % 8), (b, xl * 8 + (z + 7) % 8), (b, x_loop)]
-    sibling = (b + 1 - 2 * c, l)
+    sharers = [z_up, z_down, (b, x_loop)]
 
     def own_rows(k):
         return p_hbm.at[pl.ds(sum(SIZES[:k]), SIZES[k])]
@@ -225,7 +242,7 @@
     cent_copy.wait()
     actions = dict(
         share=share, own=lambda k: scores(k, c), sib=sibling_scores, tell=tell,
-        merge=first_merge, sums=sums,
+        merge=first_merge, sums=sums, greet=greet,
     )
     actions["pass"] = to_sibling
     for kind, k in STEPS:
@@ -278,6 +295,7 @@
             pltpu.VMEM((held, 128), jnp.float32),
             *[pltpu.VMEM((2, held, 8 * rows), jnp.float32) for rows in SIZES],
             *stats, *stats,
+            pltpu.SemaphoreType.REGULAR((GREETINGS,)),
             dma, dma,
             dma((chunks, 4)), each, each,
             each, each, each, each,

time: 49.8 us -> 49.6 us (level)
  no operation moved by 1% of the time
where the time goes in v5:
time: 49.6 us; the launch traced here: 49.5 us
  Pallas kernels  47.7 us (96%)
  local copies, waits for them, and re-layouts  0.99 us (2%)
  between operations  0.81 us (2%)
    pallas_call x1, Pallas kernels, per_device(): pl.pallas_call(functools.partial(kernel, eta), out_shape=(jax.ShapeDtypeS...  46.3 us
    pallas_call x1, Pallas kernels, per_device(): pl.pallas_call(write_out, out_shape=(jax.ShapeDtypeStruct((held, width),...  1.36 us

profile of v5, /device:TPU:1, one launch (start us, length us, event | category | flops | bytes accessed | tf_op | source)
XLA Modules:
  0.0 49.5 jit_solution(6947369208666459664)
XLA Ops:
  0.6 0.0 copy-start
  0.6 1.0 %copy-done = bf16[192,1024]{1,0:T(8,128)(2,1)S(1)} copy-done((bf16[192,1024]{1,0:T(8,128)(2,1)S(1)}, bf16[192,1024]{1,0:T(8,128)(2,1)}, u32[]{:S(2)}) %copy-start) | copy-done | bytes 393240
  1.6 46.3 %shard_map.41 = (bf16[1024,1024]{1,0:T(8,128)(2,1)S(1)}, f32[1,192]{1,0:T(1,128)S(1)}) custom-call(bf16[192,1024]{1,0:T(8,128)(2,1)S(1)} %copy-done, bf16[1024,1024]{1,0:T(8,128)(2,1)} %c_hbm.1), custom_call_target="tpu_custom_call" | custom-call | flops 12884901888 | bytes 6291456 | tf_op jit(solution)/shard_map/pallas_call | solution.py:283
  48.0 1.4 %shard_map.42 = (bf16[1024,1024]{1,0:T(8,128)(2,1)}, f32[1,192]{1,0:T(1,128)}) custom-call(bf16[1024,1024]{1,0:T(8,128)(2,1)S(1)} %get-tuple-element.6.fresh, f32[1,192]{1,0:T(1,128)S(1)} %get-tuple-element.7.norm), custom_call_target="tpu_custom_call" | custom-call | tf_op jit(solution)/shard_map/pallas_call | solution.py:311
Async XLA Ops:
  0.6 1.0 %copy-start = (bf16[192,1024]{1,0:T(8,128)(2,1)S(1)}, bf16[192,1024]{1,0:T(8,128)(2,1)}, u32[]{:S(2)}) copy-start(bf16[192,1024]{1,0:T(8,128)(2,1)} %p_hbm.1) | copy-start | bytes 1179652
